TPU v7x, 32 devices: a whole 2x2x4 slice. The times are simulated.
32 devices in a mesh: tok: 8 (over z, y), tp: 4 (over x, core).
Axes of the slice: x: 2, y: 2, z: 4, core: 2. Of those that a mesh axis runs over, the one named last changes fastest.
Arguments:
- inputs: bfloat16 [6144, 2304], P('tok'), may hold values from -7 to 7
- seq_lengths: int32 [4], replicated, may hold values from 1024 to 2048, as said below
- gain_attn_in: bfloat16 [2304], P('tok'), may hold values from 0.5 to 1.5
- gain_attn_out: bfloat16 [2304], P('tok'), may hold values from 0.5 to 1.5
- gain_ffn_in: bfloat16 [2304], P('tok'), may hold values from 0.5 to 1.5
- gain_ffn_out: bfloat16 [2304], P('tok'), may hold values from 0.5 to 1.5
- w_query: bfloat16 [2304, 2048], P('tok', 'tp'), may hold values from -2 to 2
- w_key: bfloat16 [2304, 1024], P('tok', 'tp'), may hold values from -2 to 2
- w_value: bfloat16 [2304, 1024], P('tok', 'tp'), may hold values from -0.125 to 0.125
- w_out: bfloat16 [2304, 2048], P('tok', 'tp'), may hold values from -0.125 to 0.125
- w_gate: bfloat16 [2304, 9216], P('tok', 'tp'), may hold values from -0.125 to 0.125
- w_up: bfloat16 [2304, 9216], P('tok', 'tp'), may hold values from -0.125 to 0.125
- w_down: bfloat16 [2304, 9216], P('tok', 'tp'), may hold values from -0.0625 to 0.0625
- out_grad: bfloat16 [6144, 2304], P('tok'), may hold values from -6 to 6
Outputs:
- layer_out: bfloat16 [6144, 2304], P('tok')
- input_grad: float32 [6144, 2304], P('tok')
- gain_attn_in_grad: float32 [2304], P('tok')
- gain_attn_out_grad: float32 [2304], P('tok')
- gain_ffn_in_grad: float32 [2304], P('tok')
- gain_ffn_out_grad: float32 [2304], P('tok')
- w_query_grad: float32 [2304, 2048], P('tok', 'tp')
- w_key_grad: float32 [2304, 1024], P('tok', 'tp')
- w_value_grad: float32 [2304, 1024], P('tok', 'tp')
- w_out_grad: float32 [2304, 2048], P('tok', 'tp')
- w_gate_grad: float32 [2304, 9216], P('tok', 'tp')
- w_up_grad: float32 [2304, 9216], P('tok', 'tp')
- w_down_grad: float32 [2304, 9216], P('tok', 'tp')
Inputs may be any that keep to these rules, and one draw needn't show every extreme that they name: `seq_lengths`: lengths of the 4 packed sequences in order; they sum to 6144, and entries 2k and 2k + 1 sum to 3072.
All inputs are finite; a program needn't handle non-finite values.
Results may differ from a plain program's by a relative error of at most 0.023.
Values may be sent and summed in bfloat16 or wider, within the bound.
A program may use at most 256 MiB of HBM per device.

v0:
```python
from functools import partial
import jax
import jax.numpy as jnp
from jax import lax
from jax.sharding import PartitionSpec as P

HEAD_DIM = 256
REACH = 3
softcap_limit = 50.0
norm_epsilon = 1e-06
rope_base = 10000.0
negative_fill = -1e30


def passed_along(array, axis, by):
    length = lax.axis_size(axis)
    pairs = [(i, i + by) for i in range(length) if 0 <= i + by < length]
    return lax.ppermute(array, axis, pairs)


def norm_apply(values, gain_vec):
    inverse = lax.rsqrt(jnp.mean(values * values, axis=-1, keepdims=True) + norm_epsilon)
    unit_vals = values * inverse
    return (unit_vals * gain_vec, unit_vals, inverse)


def norm_back(gradient, gain_vec, unit_vals, inverse):
    scaled = gradient * gain_vec
    input_part = inverse * (
        scaled - unit_vals * jnp.mean(scaled * unit_vals, axis=-1, keepdims=True)
    )
    return (input_part, jnp.sum(gradient * unit_vals, axis=0))


def token_places(seq_lengths, tok_index):
    starts = jnp.cumsum(seq_lengths) - seq_lengths
    passed = tok_index[:, None] >= starts[None, :]
    segment = jnp.sum(passed.astype(jnp.int32), axis=1) - 1
    seq_start = jnp.max(jnp.where(passed, starts[None, :], 0), axis=1)
    return (segment, tok_index - seq_start)


def rope_tables(position):
    half_dim = HEAD_DIM // 2
    freqs = rope_base ** (-2.0 * jnp.arange(half_dim).astype(jnp.float32) / HEAD_DIM)
    theta = position.astype(jnp.float32)[:, None] * freqs[None, :]
    return (jnp.cos(theta)[:, None, :], jnp.sin(theta)[:, None, :])


def rotate(values, cosine, sine_tab):
    half_dim = values.shape[-1] // 2
    front_half = values[..., :half_dim]
    back_half = values[..., half_dim:]
    return jnp.concatenate(
        [front_half * cosine - back_half * sine_tab, back_half * cosine + front_half * sine_tab],
        axis=-1,
    )


def rotate_back(values, cosine, sine_tab):
    half_dim = values.shape[-1] // 2
    front_half = values[..., :half_dim]
    back_half = values[..., half_dim:]
    return jnp.concatenate(
        [front_half * cosine + back_half * sine_tab, back_half * cosine - front_half * sine_tab],
        axis=-1,
    )


def fetch_window(kv_pair, offset):
    return passed_along((kv_pair[0], kv_pair[1]), "tok", offset)


def return_grads(kv_pair, offset):
    return (
        passed_along(kv_pair[0].astype(jnp.bfloat16), "tok", -offset).astype(jnp.float32),
        passed_along(kv_pair[1].astype(jnp.bfloat16), "tok", -offset).astype(jnp.float32),
    )


def contract_rows(left, right):
    return lax.dot_general(
        left, right, (((0,), (0,)), ((), ())), preferred_element_type=jnp.float32
    )


def contract_cols(left, right):
    return lax.dot_general(
        left, right, (((1,), (1,)), ((), ())), preferred_element_type=jnp.float32
    )


def local(
    inputs,
    seq_lengths,
    gain_attn_in,
    gain_attn_out,
    gain_ffn_in,
    gain_ffn_out,
    w_query,
    w_key,
    w_value,
    w_out,
    w_gate,
    w_up,
    w_down,
    out_grad,
):
    row_count = inputs.shape[0]
    head_cols = w_query.shape[1]
    kv_cols = w_key.shape[1]
    heads_local = head_cols // HEAD_DIM
    kv_local = kv_cols // HEAD_DIM
    group = heads_local // kv_local
    score_scale = HEAD_DIM ** (-0.5)
    tok_place = lax.axis_index("tok")
    own_index = tok_place * row_count + jnp.arange(row_count, dtype=jnp.int32)
    key_index = (tok_place - REACH) * row_count + jnp.arange(
        (REACH + 1) * row_count, dtype=jnp.int32
    )
    seg_query, pos_query = token_places(seq_lengths, own_index)
    seg_key, pos_key = token_places(seq_lengths, key_index)
    allowed = (seg_query[:, None] == seg_key[None, :]) & (pos_key[None, :] <= pos_query[:, None])
    cosine, sine_tab = rope_tables(pos_query)
    attn_mats = (
        lax.all_gather(w_query, "tok", axis=0, tiled=True),
        lax.all_gather(w_key, "tok", axis=0, tiled=True),
        lax.all_gather(w_value, "tok", axis=0, tiled=True),
        lax.all_gather(w_out, "tok", axis=0, tiled=True),
        lax.all_gather(gain_attn_in, "tok", axis=0, tiled=True),
        lax.all_gather(gain_attn_out, "tok", axis=0, tiled=True),
    )
    gain_one = attn_mats[4].astype(jnp.float32)
    gain_two = attn_mats[5].astype(jnp.float32)
    resid = inputs.astype(jnp.float32)
    normed_one, unit_one, inv_one = norm_apply(resid, gain_one)
    hidden_one = normed_one.astype(jnp.bfloat16)
    query_pre = jnp.dot(hidden_one, attn_mats[0], preferred_element_type=jnp.float32)
    key_pre = jnp.dot(hidden_one, attn_mats[1], preferred_element_type=jnp.float32)
    value_vec = jnp.dot(hidden_one, attn_mats[2], preferred_element_type=jnp.float32).astype(
        jnp.bfloat16
    )
    query_rot = rotate(
        query_pre.reshape(row_count, heads_local, HEAD_DIM), cosine, sine_tab
    ).astype(jnp.bfloat16)
    key_rot = (
        rotate(key_pre.reshape(row_count, kv_local, HEAD_DIM), cosine, sine_tab)
        .reshape(row_count, kv_cols)
        .astype(jnp.bfloat16)
    )
    key_parts = [key_rot]
    value_parts = [value_vec]
    for offset in range(1, REACH + 1):
        arrived = fetch_window((key_rot, value_vec), offset)
        key_parts.insert(0, arrived[0])
        value_parts.insert(0, arrived[1])
    key_grp = jnp.concatenate(key_parts, axis=0).reshape(-1, kv_local, HEAD_DIM)
    value_grp = jnp.concatenate(value_parts, axis=0).reshape(-1, kv_local, HEAD_DIM)
    query_grp = query_rot.reshape(row_count, kv_local, group, HEAD_DIM)

    def capped_scores():
        raw_scores = jnp.einsum(
            "qgjd,kgd->gjqk", query_grp, key_grp, preferred_element_type=jnp.float32
        )
        capped = softcap_limit * jnp.tanh(raw_scores * score_scale / softcap_limit)
        return (capped, jnp.where(allowed[None, None], capped, negative_fill))

    capped_fwd, masked_fwd = capped_scores()
    row_max = jnp.max(masked_fwd, axis=-1, keepdims=True)
    exponent = jnp.exp(masked_fwd - row_max)
    row_total = jnp.sum(exponent, axis=-1, keepdims=True)
    log_total = row_max + jnp.log(row_total)
    probs_low = (exponent / row_total).astype(jnp.bfloat16)
    attended = (
        jnp.einsum("gjqk,kgd->qgjd", probs_low, value_grp, preferred_element_type=jnp.float32)
        .reshape(row_count, head_cols)
        .astype(jnp.bfloat16)
    )
    attn_part = contract_cols(attended, attn_mats[3])
    attn_total = lax.psum(attn_part, "tp")
    normed_two, unit_two, inv_two = norm_apply(attn_total, gain_two)
    resid_mid = resid + normed_two
    ffn_mats = (
        lax.all_gather(w_gate, "tok", axis=0, tiled=True),
        lax.all_gather(w_up, "tok", axis=0, tiled=True),
        lax.all_gather(w_down, "tok", axis=0, tiled=True),
        lax.all_gather(gain_ffn_in, "tok", axis=0, tiled=True),
        lax.all_gather(gain_ffn_out, "tok", axis=0, tiled=True),
    )
    gain_three = ffn_mats[3].astype(jnp.float32)
    gain_four = ffn_mats[4].astype(jnp.float32)
    normed_three, unit_three, inv_three = norm_apply(resid_mid, gain_three)
    hidden_two = normed_three.astype(jnp.bfloat16)
    gate_vals = jnp.dot(hidden_two, ffn_mats[0], preferred_element_type=jnp.float32)
    up_vals = jnp.dot(hidden_two, ffn_mats[1], preferred_element_type=jnp.float32)
    gelu_tanh = partial(jax.nn.gelu, approximate=True)
    activated, gelu_pull = jax.vjp(gelu_tanh, gate_vals)
    inner = (activated * up_vals).astype(jnp.bfloat16)
    ffn_part = contract_cols(inner, ffn_mats[2])
    ffn_total = lax.psum(ffn_part, "tp")
    normed_four, unit_four, inv_four = norm_apply(ffn_total, gain_four)
    layer_out = (resid_mid + normed_four).astype(jnp.bfloat16)
    ffn_mats = (
        lax.all_gather(w_gate, "tok", axis=0, tiled=True),
        lax.all_gather(w_up, "tok", axis=0, tiled=True),
        lax.all_gather(w_down, "tok", axis=0, tiled=True),
        lax.all_gather(gain_ffn_in, "tok", axis=0, tiled=True),
        lax.all_gather(gain_ffn_out, "tok", axis=0, tiled=True),
    )
    grad_out = out_grad.astype(jnp.float32)
    d_ffn, grad_four = norm_back(grad_out, gain_four, unit_four, inv_four)
    d_ffn_low = d_ffn.astype(jnp.bfloat16)
    d_inner = jnp.dot(d_ffn_low, ffn_mats[2], preferred_element_type=jnp.float32)
    grad_down = contract_rows(d_ffn_low, inner)
    grad_upvals = (d_inner * activated).astype(jnp.bfloat16)
    grad_gatevals = gelu_pull(d_inner * up_vals)[0].astype(jnp.bfloat16)
    grad_gate = contract_rows(hidden_two, grad_gatevals)
    grad_upmat = contract_rows(hidden_two, grad_upvals)
    d_hidden_part = contract_cols(grad_gatevals, ffn_mats[0]) + contract_cols(
        grad_upvals, ffn_mats[1]
    )
    d_hidden_two = lax.psum(d_hidden_part, "tp")
    mid_add, grad_three = norm_back(d_hidden_two, gain_three, unit_three, inv_three)
    d_mid = grad_out + mid_add
    ffn_sums = (
        lax.psum_scatter(
            grad_gate.astype(jnp.bfloat16), "tok", scatter_dimension=0, tiled=True
        ).astype(jnp.float32),
        lax.psum_scatter(
            grad_upmat.astype(jnp.bfloat16), "tok", scatter_dimension=0, tiled=True
        ).astype(jnp.float32),
        lax.psum_scatter(
            grad_down.astype(jnp.bfloat16), "tok", scatter_dimension=0, tiled=True
        ).astype(jnp.float32),
        lax.psum_scatter(
            grad_three.astype(jnp.bfloat16), "tok", scatter_dimension=0, tiled=True
        ).astype(jnp.float32),
        lax.psum_scatter(
            grad_four.astype(jnp.bfloat16), "tok", scatter_dimension=0, tiled=True
        ).astype(jnp.float32),
    )
    attn_mats = (
        lax.all_gather(w_query, "tok", axis=0, tiled=True),
        lax.all_gather(w_key, "tok", axis=0, tiled=True),
        lax.all_gather(w_value, "tok", axis=0, tiled=True),
        lax.all_gather(w_out, "tok", axis=0, tiled=True),
        lax.all_gather(gain_attn_in, "tok", axis=0, tiled=True),
        lax.all_gather(gain_attn_out, "tok", axis=0, tiled=True),
    )
    d_attn, grad_two = norm_back(d_mid, gain_two, unit_two, inv_two)
    d_attn_low = d_attn.astype(jnp.bfloat16)
    grad_outmat = contract_rows(d_attn_low, attended)
    d_attended = jnp.dot(d_attn_low, attn_mats[3], preferred_element_type=jnp.float32).astype(
        jnp.bfloat16
    )
    d_att_grp = d_attended.reshape(row_count, kv_local, group, HEAD_DIM)
    capped_bwd, masked_bwd = capped_scores()
    probs = jnp.exp(masked_bwd - log_total)
    probs_back = probs.astype(jnp.bfloat16)
    d_probs = jnp.einsum("qgjd,kgd->gjqk", d_att_grp, value_grp, preferred_element_type=jnp.float32)
    d_value_win = jnp.einsum(
        "gjqk,qgjd->kgd", probs_back, d_att_grp, preferred_element_type=jnp.float32
    )
    row_delta = jnp.sum(probs * d_probs, axis=-1, keepdims=True)
    ratio_cap = capped_bwd / softcap_limit
    d_raw = (probs * (d_probs - row_delta) * (1.0 - ratio_cap * ratio_cap) * score_scale).astype(
        jnp.bfloat16
    )
    d_query_rot = jnp.einsum("gjqk,kgd->qgjd", d_raw, key_grp, preferred_element_type=jnp.float32)
    d_key_win = jnp.einsum("gjqk,qgjd->kgd", d_raw, query_grp, preferred_element_type=jnp.float32)
    d_key_slots = d_key_win.reshape(REACH + 1, row_count, kv_cols)
    d_value_slots = d_value_win.reshape(REACH + 1, row_count, kv_cols)
    key_total = d_key_slots[REACH]
    value_total = d_value_slots[REACH]
    for offset in range(1, REACH + 1):
        arrived = return_grads((d_key_slots[REACH - offset], d_value_slots[REACH - offset]), offset)
        key_total = key_total + arrived[0]
        value_total = value_total + arrived[1]
    d_query = (
        rotate_back(d_query_rot.reshape(row_count, heads_local, HEAD_DIM), cosine, sine_tab)
        .reshape(row_count, head_cols)
        .astype(jnp.bfloat16)
    )
    d_key = (
        rotate_back(key_total.reshape(row_count, kv_local, HEAD_DIM), cosine, sine_tab)
        .reshape(row_count, kv_cols)
        .astype(jnp.bfloat16)
    )
    d_value = value_total.astype(jnp.bfloat16)
    grad_query = contract_rows(hidden_one, d_query)
    grad_key = contract_rows(hidden_one, d_key)
    grad_value = contract_rows(hidden_one, d_value)
    d_hidden_one_part = (
        contract_cols(d_query, attn_mats[0])
        + contract_cols(d_key, attn_mats[1])
        + contract_cols(d_value, attn_mats[2])
    )
    d_hidden_one = lax.psum(d_hidden_one_part.astype(jnp.bfloat16), "tp").astype(jnp.float32)
    input_add, grad_one = norm_back(d_hidden_one, gain_one, unit_one, inv_one)
    input_grad = d_mid + input_add
    attn_sums = (
        lax.psum_scatter(
            grad_query.astype(jnp.bfloat16), "tok", scatter_dimension=0, tiled=True
        ).astype(jnp.float32),
        lax.psum_scatter(
            grad_key.astype(jnp.bfloat16), "tok", scatter_dimension=0, tiled=True
        ).astype(jnp.float32),
        lax.psum_scatter(
            grad_value.astype(jnp.bfloat16), "tok", scatter_dimension=0, tiled=True
        ).astype(jnp.float32),
        lax.psum_scatter(
            grad_outmat.astype(jnp.bfloat16), "tok", scatter_dimension=0, tiled=True
        ).astype(jnp.float32),
        lax.psum_scatter(
            grad_one.astype(jnp.bfloat16), "tok", scatter_dimension=0, tiled=True
        ).astype(jnp.float32),
        lax.psum_scatter(
            grad_two.astype(jnp.bfloat16), "tok", scatter_dimension=0, tiled=True
        ).astype(jnp.float32),
    )
    return (
        layer_out,
        input_grad,
        attn_sums[4],
        attn_sums[5],
        ffn_sums[3],
        ffn_sums[4],
        attn_sums[0],
        attn_sums[1],
        attn_sums[2],
        attn_sums[3],
        ffn_sums[0],
        ffn_sums[1],
        ffn_sums[2],
    )


def solution(mesh):
    in_specs = (
        P("tok", None),
        P(),
        P("tok"),
        P("tok"),
        P("tok"),
        P("tok"),
        P("tok", "tp"),
        P("tok", "tp"),
        P("tok", "tp"),
        P("tok", "tp"),
        P("tok", "tp"),
        P("tok", "tp"),
        P("tok", "tp"),
        P("tok", None),
    )
    out_specs = (
        P("tok", None),
        P("tok", None),
        P("tok"),
        P("tok"),
        P("tok"),
        P("tok"),
        P("tok", "tp"),
        P("tok", "tp"),
        P("tok", "tp"),
        P("tok", "tp"),
        P("tok", "tp"),
        P("tok", "tp"),
        P("tok", "tp"),
    )
    return jax.shard_map(local, mesh=mesh, in_specs=in_specs, out_specs=out_specs, check_vma=False)
```

profile of v0, /device:TPU:0, one launch (start us, length us, event | category | flops | bytes accessed | tf_op | source)
XLA Modules:
  0.0 2218.1 jit_solution(15859377549336782163)
XLA Ops:
  23.4 39.7 %all-reduce.9 = (bf16[2304]{0:T(1024)(128)(2,1)}, bf16[2304]{0:T(1024)(128)(2,1)}, bf16[2304]{0:T(1024)(128)(2,1)}, bf16[2304]{0:T(1024)(128)(2,1)}) all-reduce(bf16[2304]{0:T(1024)(128)(2,1)} %dynamic-update-slice, bf16[2304]{0:T(1024)(128)(2,1)} %copy-done.40, ...), channel_id=1, replica_groups=mesh['tok'=8,'tp'=4] {'tok'}, use_global_device_ids=true, to_apply=%add | all-reduce | flops 9216 | bytes 36864
  80.0 17.7 all-gather.10.cloned.1.call-done
  113.1 49.7 %all-gather.12.cloned.1.call-done = bf16[2304,512]{1,0:T(8,128)(2,1)} async-done(((bf16[288,512]{1,0:T(8,128)(2,1)}), bf16[2304,512]{1,0:T(8,128)(2,1)}) %all-gather.12.cloned.1.call-update) | async-done | bytes 2359312 | tf_op jit(solution)/shard_map/all_gather | solution.py:126
  204.6 24.7 %all-gather.14.cloned.1.call-done = bf16[2304,512]{1,0:T(8,128)(2,1)} async-done(((bf16[288,512]{1,0:T(8,128)(2,1)}), bf16[2304,512]{1,0:T(8,128)(2,1)}) %all-gather.14.cloned.1.call-update) | async-done | bytes 2359312 | tf_op jit(solution)/shard_map/all_gather | solution.py:129
  240.4 126.9 %all-reduce.15.cloned.1.call-done = f32[768,2304]{1,0:T(8,128)} async-done(((f32[768,2304]{1,0:T(8,128)}), f32[768,2304]{1,0:T(8,128)}) %all-reduce.15.cloned.1.call-update) | async-done | bytes 7077904 | tf_op jit(solution)/shard_map/psum | solution.py:180
  378.4 143.6 %all-gather.16.cloned.1.call-done = bf16[2304,2304]{1,0:T(8,128)(2,1)} async-done(((bf16[288,2304]{1,0:T(8,128)(2,1)}), bf16[2304,2304]{1,0:T(8,128)(2,1)}) %all-gather.16.cloned.1.call-update) | async-done | bytes 10616848 | tf_op jit(solution)/shard_map/all_gather | solution.py:184
  522.1 13.8 fusion.113
  535.8 139.1 %all-gather.18.cloned.1.call-done = bf16[2304,2304]{1,0:T(8,128)(2,1)} async-done(((bf16[288,2304]{1,0:T(8,128)(2,1)}), bf16[2304,2304]{1,0:T(8,128)(2,1)}) %all-gather.18.cloned.1.call-update) | async-done | bytes 10616848 | tf_op jit(solution)/shard_map/all_gather | solution.py:185
  674.9 15.6 multiply_convert_fusion.2
  690.5 137.2 %all-gather.20.cloned.1.call-done = bf16[2304,2304]{1,0:T(8,128)(2,1)} async-done(((bf16[288,2304]{1,0:T(8,128)(2,1)}), bf16[2304,2304]{1,0:T(8,128)(2,1)}) %all-gather.20.cloned.1.call-update) | async-done | bytes 10616848 | tf_op jit(solution)/shard_map/all_gather | solution.py:186
  827.8 14.9 fusion.114
  844.2 129.2 %all-reduce.17.cloned.1.call-done = f32[768,2304]{1,0:T(8,128)} async-done(((f32[768,2304]{1,0:T(8,128)}), f32[768,2304]{1,0:T(8,128)}) %all-reduce.17.cloned.1.call-update) | async-done | bytes 7077904 | tf_op jit(solution)/shard_map/psum | solution.py:200
  986.7 20.0 multiply_convert_fusion.1
  1006.7 15.1 fusion.115
  1021.8 16.0 convolution_add_fusion
  1039.2 131.4 %all-reduce.19.cloned.1.call-done = f32[768,2304]{1,0:T(8,128)} async-done(((f32[768,2304]{1,0:T(8,128)}), f32[768,2304]{1,0:T(8,128)}) %all-reduce.19.cloned.1.call-update) | async-done | bytes 7077904 | tf_op jit(solution)/shard_map/psum | solution.py:222
  1194.5 12.6 fusion.111
  1210.8 17.6 fusion.2
  1228.4 15.2 fusion.1
  1262.3 13.7 collective-permute-done.6
  1317.2 13.7 convolution_convert_fusion.1
  1331.0 13.7 convolution_convert_fusion.2
  1345.0 13.6 convolution_convert_fusion
  1359.3 21.9 all-reduce.21.cloned.1.call-done
  1385.9 38.7 %all-reduce.8 = (bf16[2304]{0:T(1024)(128)(2,1)}, bf16[2304]{0:T(1024)(128)(2,1)}, bf16[2304]{0:T(1024)(128)(2,1)}, bf16[2304]{0:T(1024)(128)(2,1)}) all-reduce(bf16[2304]{0:T(1024)(128)(2,1)} %get-tuple-element.19, bf16[2304]{0:T(1024)(128)(2,1)} %get-tuple-element.15, ...), channel_id=2, replica_groups=mesh['tok'=8,'tp'=4] {'tok'}, use_global_device_ids=true, to_apply=%region_21.22.clone | all-reduce | flops 9216 | bytes 36864
  1437.5 11.3 reduce-scatter.12.cloned.1.call-done
  1450.4 65.4 %reduce-scatter.10.cloned.1.call-done = bf16[288,256]{1,0:T(8,128)(2,1)} async-done(((bf16[2304,256]{1,0:T(8,128)(2,1)}), bf16[288,256]{1,0:T(8,128)(2,1)}) %reduce-scatter.10.cloned.1.call-update) | async-done | bytes 147472 | tf_op jit(solution)/shard_map/reduce_scatter | solution.py:305
  1517.4 70.4 %reduce-scatter.14.cloned.1.call-done = bf16[288,512]{1,0:T(8,128)(2,1)} async-done(((bf16[2304,512]{1,0:T(8,128)(2,1)}), bf16[288,512]{1,0:T(8,128)(2,1)}) %reduce-scatter.14.cloned.1.call-update) | async-done | bytes 294928 | tf_op jit(solution)/shard_map/reduce_scatter | solution.py:311
  1589.7 70.1 %reduce-scatter.8.cloned.1.call-done = bf16[288,512]{1,0:T(8,128)(2,1)} async-done(((bf16[2304,512]{1,0:T(8,128)(2,1)}), bf16[288,512]{1,0:T(8,128)(2,1)}) %reduce-scatter.8.cloned.1.call-update) | async-done | bytes 294928 | tf_op jit(solution)/shard_map/reduce_scatter | solution.py:302
  1661.6 180.7 %reduce-scatter.18.cloned.1.call-done = bf16[288,2304]{1,0:T(8,128)(2,1)} async-done(((bf16[2304,2304]{1,0:T(8,128)(2,1)}), bf16[288,2304]{1,0:T(8,128)(2,1)}) %reduce-scatter.18.cloned.1.call-update) | async-done | bytes 1327120 | tf_op jit(solution)/shard_map/reduce_scatter | solution.py:229
  1845.3 180.0 %reduce-scatter.16.cloned.1.call-done = bf16[288,2304]{1,0:T(8,128)(2,1)} async-done(((bf16[2304,2304]{1,0:T(8,128)(2,1)}), bf16[288,2304]{1,0:T(8,128)(2,1)}) %reduce-scatter.16.cloned.1.call-update) | async-done | bytes 1327120 | tf_op jit(solution)/shard_map/reduce_scatter | solution.py:226
  2028.3 179.5 %reduce-scatter.20.cloned.1.call-done = bf16[288,2304]{1,0:T(8,128)(2,1)} async-done(((bf16[2304,2304]{1,0:T(8,128)(2,1)}), bf16[288,2304]{1,0:T(8,128)(2,1)}) %reduce-scatter.20.cloned.1.call-update) | async-done | bytes 1327120 | tf_op jit(solution)/shard_map/reduce_scatter | solution.py:232
  (254 shorter events, 248.5 us)
Async XLA Ops:
  7.2 65.5 %all-gather.8.cloned.1.call-start = ((), (), s32[]{:S(2)}) async-start(), calls=%async_computation.7 | async-start | bytes 1327104 | tf_op jit(solution)/shard_map/all_gather | solution.py:128
  7.9 89.8 %all-gather.10.cloned.1.call-start = ((), (), s32[]{:S(2)}) async-start(), calls=%async_computation.8 | async-start | bytes 1327104 | tf_op jit(solution)/shard_map/all_gather | solution.py:127
  8.7 154.2 %all-gather.12.cloned.1.call-start = ((), (), s32[]{:S(2)}) async-start(), calls=%async_computation.9 | async-start | bytes 2654208 | tf_op jit(solution)/shard_map/all_gather | solution.py:126
  9.4 219.9 %all-gather.14.cloned.1.call-start = ((), (), s32[]{:S(2)}) async-start(), calls=%async_computation.10 | async-start | bytes 2654208 | tf_op jit(solution)/shard_map/all_gather | solution.py:129
  10.0 357.3 %all-reduce.15.cloned.1.call-start = ((), (), s32[]{:S(2)}) async-start(), calls=%async_computation.11 | async-start | bytes 14155776 | tf_op jit(solution)/shard_map/psum | solution.py:180
  75.8 117.1 %collective-permute-start.2 = (bf16[768,256]{1,0:T(8,128)(2,1)}, bf16[768,256]{1,0:T(8,128)(2,1)}, u32[]{:S(2)}, u32[]{:S(2)}) collective-permute-start(bf16[768,256]{1,0:T(8,128)(2,1)} %convolution_convert_fusion.8), channel_id=1, source_target_pairs={{0,4},{4,8},{8,12},{12,16},{16,20},{20,24},{24,28},{1,5},{5,9},{9,... | collective-permute-start | bytes 1179656 | tf_op jit(solution)/shard_map/ppermute | solution.py:18
  77.9 115.0 %collective-permute-start.1 = (bf16[768,256]{1,0:T(8,128)(2,1)}, bf16[768,256]{1,0:T(8,128)(2,1)}, u32[]{:S(2)}, u32[]{:S(2)}) collective-permute-start(bf16[768,256]{1,0:T(8,128)(2,1)} %convolution_convert_fusion.8), channel_id=1, source_target_pairs={{0,8},{4,12},{8,16},{12,20},{16,24},{20,28},{1,9},{5,13},{9,17},{1... | collective-permute-start | bytes 1179656 | tf_op jit(solution)/shard_map/ppermute | solution.py:18
  102.8 65.9 %collective-permute-start.5 = (bf16[768,256]{0,1:T(8,128)(2,1)}, bf16[768,256]{0,1:T(8,128)(2,1)}, u32[]{:S(2)}, u32[]{:S(2)}) collective-permute-start(bf16[768,256]{0,1:T(8,128)(2,1)} %maximum_bitcast_fusion.6), channel_id=1, source_target_pairs={{0,4},{4,8},{8,12},{12,16},{16,20},{20,24},{24,28},{1,5},{5,9},{9,... | collective-permute-start | bytes 1179656 | tf_op jit(solution)/shard_map/ppermute | solution.py:18
  105.7 72.3 %collective-permute-start.4 = (bf16[768,256]{0,1:T(8,128)(2,1)}, bf16[768,256]{0,1:T(8,128)(2,1)}, u32[]{:S(2)}, u32[]{:S(2)}) collective-permute-start(bf16[768,256]{0,1:T(8,128)(2,1)} %maximum_bitcast_fusion.6), channel_id=1, source_target_pairs={{0,8},{4,12},{8,16},{12,20},{16,24},{20,28},{1,9},{5,13},{9,17},{1... | collective-permute-start | bytes 1179656 | tf_op jit(solution)/shard_map/ppermute | solution.py:18
  110.1 68.0 %collective-permute-start.3 = (bf16[768,256]{0,1:T(8,128)(2,1)}, bf16[768,256]{0,1:T(8,128)(2,1)}, u32[]{:S(2)}, u32[]{:S(2)}) collective-permute-start(bf16[768,256]{0,1:T(8,128)(2,1)} %maximum_bitcast_fusion.6), channel_id=1, source_target_pairs={{0,12},{4,16},{8,20},{12,24},{16,28},{1,13},{5,17},{9,21},{13,25},... | collective-permute-start | bytes 1179656 | tf_op jit(solution)/shard_map/ppermute | solution.py:18
  168.7 24.9 %collective-permute-start = (bf16[768,256]{1,0:T(8,128)(2,1)}, bf16[768,256]{1,0:T(8,128)(2,1)S(1)}, u32[]{:S(2)}, u32[]{:S(2)}) collective-permute-start(bf16[768,256]{1,0:T(8,128)(2,1)} %convolution_convert_fusion.8), channel_id=1, source_target_pairs={{0,12},{4,16},{8,20},{12,24},{16,28},{1,13},{5,17},{9,21},{13,25},... | collective-permute-start | bytes 1179656 | tf_op jit(solution)/shard_map/ppermute | solution.py:18
  236.3 134.7 %copy-start.6 = (bf16[768,2304]{1,0:T(8,128)(2,1)S(1)}, bf16[768,2304]{1,0:T(8,128)(2,1)}, u32[]{:S(2)}) copy-start(bf16[768,2304]{1,0:T(8,128)(2,1)} %param.14) | copy-start | bytes 10616836
  236.3 285.8 %all-gather.16.cloned.1.call-start = ((), (), s32[]{:S(2)}) async-start(), calls=%async_computation.12 | async-start | bytes 11943936 | tf_op jit(solution)/shard_map/all_gather | solution.py:184
  236.9 438.1 %all-gather.18.cloned.1.call-start = ((), (), s32[]{:S(2)}) async-start(), calls=%async_computation.13 | async-start | bytes 11943936 | tf_op jit(solution)/shard_map/all_gather | solution.py:185
  237.6 590.2 %all-gather.20.cloned.1.call-start = ((), (), s32[]{:S(2)}) async-start(), calls=%async_computation.14 | async-start | bytes 11943936 | tf_op jit(solution)/shard_map/all_gather | solution.py:186
  238.4 735.1 %all-reduce.17.cloned.1.call-start = ((), (), s32[]{:S(2)}) async-start(), calls=%async_computation.15 | async-start | bytes 14155776 | tf_op jit(solution)/shard_map/psum | solution.py:200
  378.4 296.5 %copy-start.13 = (bf16[768,2304]{1,0:T(8,128)(2,1)}, bf16[768,2304]{1,0:T(8,128)(2,1)S(1)}, u32[]{:S(2)}) copy-start(bf16[768,2304]{1,0:T(8,128)(2,1)S(1)} %multiply_convert_fusion.3) | copy-start | bytes 10616836
  842.7 327.9 %all-reduce.19.cloned.1.call-start = ((), (), s32[]{:S(2)}) async-start(), calls=%async_computation.16 | async-start | bytes 14155776 | tf_op jit(solution)/shard_map/psum | solution.py:222
  1037.8 343.3 %all-reduce.21.cloned.1.call-start = ((), (), s32[]{:S(2)}) async-start(), calls=%async_computation.17 | async-start | bytes 7077888 | tf_op jit(solution)/shard_map/psum | solution.py:298
  1208.2 76.9 %collective-permute-start.9 = (bf16[768,256]{0,1:T(8,128)(2,1)}, bf16[768,256]{0,1:T(8,128)(2,1)S(1)}, u32[]{:S(2)}, u32[]{:S(2)}) collective-permute-start(bf16[768,256]{0,1:T(8,128)(2,1)} %get-tuple-element.46), channel_id=1, source_target_pairs={{4,0},{8,4},{12,8},{16,12},{20,16},{24,20},{28,24},{5,1},{9,5},{13... | collective-permute-start | bytes 1179656 | tf_op jit(solution)/shard_map/ppermute | solution.py:18
  1209.5 75.7 %collective-permute-start.11 = (bf16[768,256]{0,1:T(8,128)(2,1)}, bf16[768,256]{0,1:T(8,128)(2,1)}, u32[]{:S(2)}, u32[]{:S(2)}) collective-permute-start(bf16[768,256]{0,1:T(8,128)(2,1)} %get-tuple-element.47), channel_id=1, source_target_pairs={{12,0},{16,4},{20,8},{24,12},{28,16},{13,1},{17,5},{21,9},{25,13},... | collective-permute-start | bytes 1179656 | tf_op jit(solution)/shard_map/ppermute | solution.py:18
  1254.3 21.7 collective-permute-start.6
  1255.7 21.5 collective-permute-start.8
  1257.0 23.9 %collective-permute-start.7 = (bf16[768,256]{0,1:T(8,128)(2,1)S(1)}, bf16[768,256]{0,1:T(8,128)(2,1)S(1)}, u32[]{:S(2)}, u32[]{:S(2)}) collective-permute-start(bf16[768,256]{0,1:T(8,128)(2,1)S(1)} %get-tuple-element.51), channel_id=1, source_target_pairs={{8,0},{12,4},{16,8},{20,12},{24,16},{28,20},{9,1},{13,5},{17,9},{2... | collective-permute-start | bytes 1179656 | tf_op jit(solution)/shard_map/ppermute | solution.py:18
  1276.0 18.0 collective-permute-start.10
  1299.1 149.7 %reduce-scatter.12.cloned.1.call-start = ((), (), s32[]{:S(2)}) async-start(), calls=%async_computation.20 | async-start | bytes 1327104 | tf_op jit(solution)/shard_map/reduce_scatter | solution.py:308
  1302.7 213.1 %reduce-scatter.10.cloned.1.call-start = ((), (), s32[]{:S(2)}) async-start(), calls=%async_computation.19 | async-start | bytes 1327104 | tf_op jit(solution)/shard_map/reduce_scatter | solution.py:305
  1306.2 281.6 %reduce-scatter.14.cloned.1.call-start = ((), (), s32[]{:S(2)}) async-start(), calls=%async_computation.21 | async-start | bytes 2654208 | tf_op jit(solution)/shard_map/reduce_scatter | solution.py:311
  1312.0 347.8 %reduce-scatter.8.cloned.1.call-start = ((), (), s32[]{:S(2)}) async-start(), calls=%async_computation.18 | async-start | bytes 2654208 | tf_op jit(solution)/shard_map/reduce_scatter | solution.py:302
  1317.1 525.2 %reduce-scatter.18.cloned.1.call-start = ((), (), s32[]{:S(2)}) async-start(), calls=%async_computation.23 | async-start | bytes 11943936 | tf_op jit(solution)/shard_map/reduce_scatter | solution.py:229
  1330.9 694.3 %reduce-scatter.16.cloned.1.call-start = ((), (), s32[]{:S(2)}) async-start(), calls=%async_computation.22 | async-start | bytes 11943936 | tf_op jit(solution)/shard_map/reduce_scatter | solution.py:226
  1344.7 863.2 %reduce-scatter.20.cloned.1.call-start = ((), (), s32[]{:S(2)}) async-start(), calls=%async_computation.24 | async-start | bytes 11943936 | tf_op jit(solution)/shard_map/reduce_scatter | solution.py:232
  (50 other events, 791.0 us)
Sparse Core Ops, SparseCore 0:
  10.2 43.9 all-gather.7
  56.4 41.2 all-gather.9
  99.9 62.8 all-gather.11
  164.9 64.4 all-gather.13
  236.4 130.8 all-reduce.14
  369.3 152.6 all-gather.15
  524.2 150.6 all-gather.17
  677.1 150.6 all-gather.19
  842.8 130.5 all-reduce.16
  1038.0 132.5 all-reduce.18
  1299.3 81.8 all-reduce.20
  1384.4 64.3 reduce-scatter.11
  1452.8 62.9 reduce-scatter.9
  1519.7 68.0 reduce-scatter.13
  1591.8 67.9 reduce-scatter.7
  1663.2 179.0 reduce-scatter.17
  1846.2 179.0 reduce-scatter.15
  2028.7 179.0 reduce-scatter.19
where the time goes:
time: 2230 us; the launch traced here: 2220 us
  waiting for transfers between devices  1710 us (77%)
  matrix products  240 us (11%)
  other arithmetic  123 us (6%)
  blocking collectives  78.4 us (4%)
  starting transfers between devices  32.9 us (1%)
    reduce_scatter x1, waiting for transfers between devices, local(): lax.psum_scatter(grad_upmat.astype(jnp.bfloat16), 'tok', scatter_dimensio...  181 us
    reduce_scatter x1, waiting for transfers between devices, local(): lax.psum_scatter(grad_gate.astype(jnp.bfloat16), 'tok', scatter_dimension...  180 us
    reduce_scatter x1, waiting for transfers between devices, local(): lax.psum_scatter(grad_down.astype(jnp.bfloat16), 'tok', scatter_dimension...  180 us
    all_gather x1, waiting for transfers between devices, local(): lax.all_gather(w_gate, 'tok', axis=0, tiled=True)  144 us
    all_gather x1, waiting for transfers between devices, local(): lax.all_gather(w_up, 'tok', axis=0, tiled=True)  139 us
    all_gather x1, waiting for transfers between devices, local(): lax.all_gather(w_down, 'tok', axis=0, tiled=True)  137 us
    psum x1, waiting for transfers between devices, local(): d_hidden_two = lax.psum(d_hidden_part, 'tp')  131 us
    psum x1, waiting for transfers between devices, local(): ffn_total = lax.psum(ffn_part, 'tp')  129 us
  transfers between devices with their start and end apart: 30, of which 21 were waited for; matrix products, arithmetic and copies ran while one was open for 11% of the time, Pallas kernels for 0%

commit v1 on v0

--- a/solution.py
+++ b/solution.py
@@ -3,6 +3,7 @@
 import jax.numpy as jnp
 from jax import lax
 from jax.sharding import PartitionSpec as P
+from jax.lax import all_gather
 
 HEAD_DIM = 256
 REACH = 3
@@ -177,7 +178,12 @@
         .astype(jnp.bfloat16)
     )
     attn_part = contract_cols(attended, attn_mats[3])
-    attn_total = lax.psum(attn_part, "tp")
+
+    def _press_widths(xs):
+        t1 = all_gather(xs, "tp")
+        return jnp.sum(t1, axis=0)
+
+    attn_total = _press_widths(attn_part)
     normed_two, unit_two, inv_two = norm_apply(attn_total, gain_two)
     resid_mid = resid + normed_two
     ffn_mats = (

time: 2230 us -> 2270 us (1.018)
  waiting for transfers between devices: 1710 us -> 1740 us
    all_gather x0 -> x1, waiting for transfers between devices: none -> 168 us  [_press_widths(): t1 = all_gather(xs, 'tp')]
    psum x1 -> x0, waiting for transfers between devices: 127 us -> none  [local(): attn_total = lax.psum(attn_part, 'tp')]
where the time goes in v1:
time: 2270 us; the launch traced here: 2260 us
  waiting for transfers between devices  1740 us (77%)
  matrix products  240 us (11%)
  other arithmetic  136 us (6%)
  blocking collectives  78.4 us (3%)
  starting transfers between devices  33.3 us (1%)
    reduce_scatter x1, waiting for transfers between devices, local(): lax.psum_scatter(grad_upmat.astype(jnp.bfloat16), 'tok', scatter_dimensio...  181 us
    reduce_scatter x1, waiting for transfers between devices, local(): lax.psum_scatter(grad_gate.astype(jnp.bfloat16), 'tok', scatter_dimension...  180 us
    reduce_scatter x1, waiting for transfers between devices, local(): lax.psum_scatter(grad_down.astype(jnp.bfloat16), 'tok', scatter_dimension...  180 us
    all_gather x1, waiting for transfers between devices, _press_widths(): t1 = all_gather(xs, 'tp')  168 us
    all_gather x1, waiting for transfers between devices, local(): lax.all_gather(w_up, 'tok', axis=0, tiled=True)  139 us
    all_gather x1, waiting for transfers between devices, local(): lax.all_gather(w_down, 'tok', axis=0, tiled=True)  137 us
    psum x1, waiting for transfers between devices, local(): d_hidden_two = lax.psum(d_hidden_part, 'tp')  131 us
    all_gather x1, waiting for transfers between devices, local(): lax.all_gather(w_gate, 'tok', axis=0, tiled=True)  129 us
  transfers between devices with their start and end apart: 30, of which 21 were waited for; matrix products, arithmetic and copies ran while one was open for 11% of the time, Pallas kernels for 0%

profile of v1, /device:TPU:0, one launch (start us, length us, event | category | flops | bytes accessed | tf_op | source)
XLA Modules:
  0.0 2257.8 jit_solution(14844756217184954062)
XLA Ops:
  23.4 39.7 %all-reduce.9 = (bf16[2304]{0:T(1024)(128)(2,1)}, bf16[2304]{0:T(1024)(128)(2,1)}, bf16[2304]{0:T(1024)(128)(2,1)}, bf16[2304]{0:T(1024)(128)(2,1)}) all-reduce(bf16[2304]{0:T(1024)(128)(2,1)} %dynamic-update-slice, bf16[2304]{0:T(1024)(128)(2,1)} %copy-done.40, ...), channel_id=1, replica_groups=mesh['tok'=8,'tp'=4] {'tok'}, use_global_device_ids=true, to_apply=%add | all-reduce | flops 9216 | bytes 36864
  80.0 17.8 all-gather.12.cloned.1.call-done
  113.1 49.7 %all-gather.14.cloned.1.call-done = bf16[2304,512]{1,0:T(8,128)(2,1)} async-done(((bf16[288,512]{1,0:T(8,128)(2,1)}), bf16[2304,512]{1,0:T(8,128)(2,1)}) %all-gather.14.cloned.1.call-update) | async-done | bytes 2359312 | tf_op jit(solution)/shard_map/all_gather | solution.py:127
  204.6 24.7 %all-gather.16.cloned.1.call-done = bf16[2304,512]{1,0:T(8,128)(2,1)} async-done(((bf16[288,512]{1,0:T(8,128)(2,1)}), bf16[2304,512]{1,0:T(8,128)(2,1)}) %all-gather.16.cloned.1.call-update) | async-done | bytes 2359312 | tf_op jit(solution)/shard_map/all_gather | solution.py:130
  239.0 168.1 %all-gather.24.cloned.1.call-done = f32[3072,2304]{1,0:T(8,128)} async-done(((f32[768,2304]{1,0:T(8,128)}), f32[3072,2304]{1,0:T(8,128)}) %all-gather.24.cloned.1.call-update) | async-done | bytes 28311568 | tf_op jit(solution)/shard_map/all_gather | solution.py:183
  407.2 14.8 reduce_sum.157
  432.4 129.3 %all-gather.18.cloned.1.call-done = bf16[2304,2304]{1,0:T(8,128)(2,1)} async-done(((bf16[288,2304]{1,0:T(8,128)(2,1)}), bf16[2304,2304]{1,0:T(8,128)(2,1)}) %all-gather.18.cloned.1.call-update) | async-done | bytes 10616848 | tf_op jit(solution)/shard_map/all_gather | solution.py:190
  561.7 13.8 fusion.113
  575.5 139.1 %all-gather.20.cloned.1.call-done = bf16[2304,2304]{1,0:T(8,128)(2,1)} async-done(((bf16[288,2304]{1,0:T(8,128)(2,1)}), bf16[2304,2304]{1,0:T(8,128)(2,1)}) %all-gather.20.cloned.1.call-update) | async-done | bytes 10616848 | tf_op jit(solution)/shard_map/all_gather | solution.py:191
  714.5 15.6 multiply_convert_fusion.2
  730.1 137.3 %all-gather.22.cloned.1.call-done = bf16[2304,2304]{1,0:T(8,128)(2,1)} async-done(((bf16[288,2304]{1,0:T(8,128)(2,1)}), bf16[2304,2304]{1,0:T(8,128)(2,1)}) %all-gather.22.cloned.1.call-update) | async-done | bytes 10616848 | tf_op jit(solution)/shard_map/all_gather | solution.py:192
  867.4 15.1 fusion.114
  884.0 129.2 %all-reduce.14.cloned.1.call-done = f32[768,2304]{1,0:T(8,128)} async-done(((f32[768,2304]{1,0:T(8,128)}), f32[768,2304]{1,0:T(8,128)}) %all-reduce.14.cloned.1.call-update) | async-done | bytes 7077904 | tf_op jit(solution)/shard_map/psum | solution.py:206
  1026.5 20.0 multiply_convert_fusion.1
  1046.5 15.2 fusion.115
  1061.7 16.0 convolution_add_fusion
  1079.1 131.4 %all-reduce.16.cloned.1.call-done = f32[768,2304]{1,0:T(8,128)} async-done(((f32[768,2304]{1,0:T(8,128)}), f32[768,2304]{1,0:T(8,128)}) %all-reduce.16.cloned.1.call-update) | async-done | bytes 7077904 | tf_op jit(solution)/shard_map/psum | solution.py:228
  1234.6 12.6 fusion.111
  1250.9 17.4 fusion.2
  1268.3 15.3 fusion.1
  1302.3 13.6 collective-permute-done.6
  1357.3 13.7 convolution_convert_fusion.1
  1371.0 13.6 convolution_convert_fusion.2
  1384.9 13.6 convolution_convert_fusion
  1399.2 21.9 all-reduce.18.cloned.1.call-done
  1425.8 38.7 %all-reduce.8 = (bf16[2304]{0:T(1024)(128)(2,1)}, bf16[2304]{0:T(1024)(128)(2,1)}, bf16[2304]{0:T(1024)(128)(2,1)}, bf16[2304]{0:T(1024)(128)(2,1)}) all-reduce(bf16[2304]{0:T(1024)(128)(2,1)} %get-tuple-element.19, bf16[2304]{0:T(1024)(128)(2,1)} %get-tuple-element.15, ...), channel_id=3, replica_groups=mesh['tok'=8,'tp'=4] {'tok'}, use_global_device_ids=true, to_apply=%region_21.22.clone | all-reduce | flops 9216 | bytes 36864
  1490.4 65.3 %reduce-scatter.10.cloned.1.call-done = bf16[288,256]{1,0:T(8,128)(2,1)} async-done(((bf16[2304,256]{1,0:T(8,128)(2,1)}), bf16[288,256]{1,0:T(8,128)(2,1)}) %reduce-scatter.10.cloned.1.call-update) | async-done | bytes 147472 | tf_op jit(solution)/shard_map/reduce_scatter | solution.py:311
  1557.3 70.4 %reduce-scatter.14.cloned.1.call-done = bf16[288,512]{1,0:T(8,128)(2,1)} async-done(((bf16[2304,512]{1,0:T(8,128)(2,1)}), bf16[288,512]{1,0:T(8,128)(2,1)}) %reduce-scatter.14.cloned.1.call-update) | async-done | bytes 294928 | tf_op jit(solution)/shard_map/reduce_scatter | solution.py:317
  1629.6 70.3 %reduce-scatter.8.cloned.1.call-done = bf16[288,512]{1,0:T(8,128)(2,1)} async-done(((bf16[2304,512]{1,0:T(8,128)(2,1)}), bf16[288,512]{1,0:T(8,128)(2,1)}) %reduce-scatter.8.cloned.1.call-update) | async-done | bytes 294928 | tf_op jit(solution)/shard_map/reduce_scatter | solution.py:308
  1701.8 180.7 %reduce-scatter.18.cloned.1.call-done = bf16[288,2304]{1,0:T(8,128)(2,1)} async-done(((bf16[2304,2304]{1,0:T(8,128)(2,1)}), bf16[288,2304]{1,0:T(8,128)(2,1)}) %reduce-scatter.18.cloned.1.call-update) | async-done | bytes 1327120 | tf_op jit(solution)/shard_map/reduce_scatter | solution.py:235
  1885.4 179.8 %reduce-scatter.16.cloned.1.call-done = bf16[288,2304]{1,0:T(8,128)(2,1)} async-done(((bf16[2304,2304]{1,0:T(8,128)(2,1)}), bf16[288,2304]{1,0:T(8,128)(2,1)}) %reduce-scatter.16.cloned.1.call-update) | async-done | bytes 1327120 | tf_op jit(solution)/shard_map/reduce_scatter | solution.py:232
  2068.2 179.5 %reduce-scatter.20.cloned.1.call-done = bf16[288,2304]{1,0:T(8,128)(2,1)} async-done(((bf16[2304,2304]{1,0:T(8,128)(2,1)}), bf16[288,2304]{1,0:T(8,128)(2,1)}) %reduce-scatter.20.cloned.1.call-update) | async-done | bytes 1327120 | tf_op jit(solution)/shard_map/reduce_scatter | solution.py:238
  (259 shorter events, 258.0 us)
Async XLA Ops:
  7.2 65.5 %all-gather.10.cloned.1.call-start = ((), (), s32[]{:S(2)}) async-start(), calls=%async_computation.7 | async-start | bytes 1327104 | tf_op jit(solution)/shard_map/all_gather | solution.py:129
  7.9 89.8 %all-gather.12.cloned.1.call-start = ((), (), s32[]{:S(2)}) async-start(), calls=%async_computation.8 | async-start | bytes 1327104 | tf_op jit(solution)/shard_map/all_gather | solution.py:128
  8.7 154.1 %all-gather.14.cloned.1.call-start = ((), (), s32[]{:S(2)}) async-start(), calls=%async_computation.9 | async-start | bytes 2654208 | tf_op jit(solution)/shard_map/all_gather | solution.py:127
  9.4 219.9 %all-gather.16.cloned.1.call-start = ((), (), s32[]{:S(2)}) async-start(), calls=%async_computation.10 | async-start | bytes 2654208 | tf_op jit(solution)/shard_map/all_gather | solution.py:130
  10.0 397.2 %all-gather.24.cloned.1.call-start = ((), (), s32[]{:S(2)}) async-start(), calls=%async_computation.24 | async-start | bytes 35389440 | tf_op jit(solution)/shard_map/all_gather | solution.py:183
  75.8 117.3 %collective-permute-start.2 = (bf16[768,256]{1,0:T(8,128)(2,1)}, bf16[768,256]{1,0:T(8,128)(2,1)}, u32[]{:S(2)}, u32[]{:S(2)}) collective-permute-start(bf16[768,256]{1,0:T(8,128)(2,1)} %convolution_convert_fusion.8), channel_id=1, source_target_pairs={{0,4},{4,8},{8,12},{12,16},{16,20},{20,24},{24,28},{1,5},{5,9},{9,... | collective-permute-start | bytes 1179656 | tf_op jit(solution)/shard_map/ppermute | solution.py:19
  77.9 115.3 %collective-permute-start.1 = (bf16[768,256]{1,0:T(8,128)(2,1)}, bf16[768,256]{1,0:T(8,128)(2,1)}, u32[]{:S(2)}, u32[]{:S(2)}) collective-permute-start(bf16[768,256]{1,0:T(8,128)(2,1)} %convolution_convert_fusion.8), channel_id=1, source_target_pairs={{0,8},{4,12},{8,16},{12,20},{16,24},{20,28},{1,9},{5,13},{9,17},{1... | collective-permute-start | bytes 1179656 | tf_op jit(solution)/shard_map/ppermute | solution.py:19
  102.8 65.9 %collective-permute-start.5 = (bf16[768,256]{0,1:T(8,128)(2,1)}, bf16[768,256]{0,1:T(8,128)(2,1)}, u32[]{:S(2)}, u32[]{:S(2)}) collective-permute-start(bf16[768,256]{0,1:T(8,128)(2,1)} %maximum_bitcast_fusion.6), channel_id=1, source_target_pairs={{0,4},{4,8},{8,12},{12,16},{16,20},{20,24},{24,28},{1,5},{5,9},{9,... | collective-permute-start | bytes 1179656 | tf_op jit(solution)/shard_map/ppermute | solution.py:19
  105.7 72.6 %collective-permute-start.4 = (bf16[768,256]{0,1:T(8,128)(2,1)}, bf16[768,256]{0,1:T(8,128)(2,1)}, u32[]{:S(2)}, u32[]{:S(2)}) collective-permute-start(bf16[768,256]{0,1:T(8,128)(2,1)} %maximum_bitcast_fusion.6), channel_id=1, source_target_pairs={{0,8},{4,12},{8,16},{12,20},{16,24},{20,28},{1,9},{5,13},{9,17},{1... | collective-permute-start | bytes 1179656 | tf_op jit(solution)/shard_map/ppermute | solution.py:19
  110.1 68.2 %collective-permute-start.3 = (bf16[768,256]{0,1:T(8,128)(2,1)}, bf16[768,256]{0,1:T(8,128)(2,1)}, u32[]{:S(2)}, u32[]{:S(2)}) collective-permute-start(bf16[768,256]{0,1:T(8,128)(2,1)} %maximum_bitcast_fusion.6), channel_id=1, source_target_pairs={{0,12},{4,16},{8,20},{12,24},{16,28},{1,13},{5,17},{9,21},{13,25},... | collective-permute-start | bytes 1179656 | tf_op jit(solution)/shard_map/ppermute | solution.py:19
  168.7 24.8 %collective-permute-start = (bf16[768,256]{1,0:T(8,128)(2,1)}, bf16[768,256]{1,0:T(8,128)(2,1)S(1)}, u32[]{:S(2)}, u32[]{:S(2)}) collective-permute-start(bf16[768,256]{1,0:T(8,128)(2,1)} %convolution_convert_fusion.8), channel_id=1, source_target_pairs={{0,12},{4,16},{8,20},{12,24},{16,28},{1,13},{5,17},{9,21},{13,25},... | collective-permute-start | bytes 1179656 | tf_op jit(solution)/shard_map/ppermute | solution.py:19
  236.3 325.4 %all-gather.18.cloned.1.call-start = ((), (), s32[]{:S(2)}) async-start(), calls=%async_computation.11 | async-start | bytes 11943936 | tf_op jit(solution)/shard_map/all_gather | solution.py:190
  236.8 477.7 %all-gather.20.cloned.1.call-start = ((), (), s32[]{:S(2)}) async-start(), calls=%async_computation.12 | async-start | bytes 11943936 | tf_op jit(solution)/shard_map/all_gather | solution.py:191
  237.6 629.8 %all-gather.22.cloned.1.call-start = ((), (), s32[]{:S(2)}) async-start(), calls=%async_computation.13 | async-start | bytes 11943936 | tf_op jit(solution)/shard_map/all_gather | solution.py:192
  238.3 774.9 %all-reduce.14.cloned.1.call-start = ((), (), s32[]{:S(2)}) async-start(), calls=%async_computation.14 | async-start | bytes 14155776 | tf_op jit(solution)/shard_map/psum | solution.py:206
  432.4 282.1 %copy-start.13 = (bf16[768,2304]{1,0:T(8,128)(2,1)}, bf16[768,2304]{1,0:T(8,128)(2,1)S(1)}, u32[]{:S(2)}) copy-start(bf16[768,2304]{1,0:T(8,128)(2,1)S(1)} %multiply_convert_fusion.3) | copy-start | bytes 10616836
  882.5 134.5 %copy-start.8 = (bf16[768,2304]{1,0:T(8,128)(2,1)S(1)}, bf16[768,2304]{1,0:T(8,128)(2,1)}, u32[]{:S(2)}) copy-start(bf16[768,2304]{1,0:T(8,128)(2,1)} %param.27) | copy-start | bytes 10616836
  882.6 327.9 %all-reduce.16.cloned.1.call-start = ((), (), s32[]{:S(2)}) async-start(), calls=%async_computation.15 | async-start | bytes 14155776 | tf_op jit(solution)/shard_map/psum | solution.py:228
  1077.7 343.4 %all-reduce.18.cloned.1.call-start = ((), (), s32[]{:S(2)}) async-start(), calls=%async_computation.16 | async-start | bytes 7077888 | tf_op jit(solution)/shard_map/psum | solution.py:304
  1248.3 76.8 %collective-permute-start.9 = (bf16[768,256]{0,1:T(8,128)(2,1)}, bf16[768,256]{0,1:T(8,128)(2,1)S(1)}, u32[]{:S(2)}, u32[]{:S(2)}) collective-permute-start(bf16[768,256]{0,1:T(8,128)(2,1)} %get-tuple-element.46), channel_id=1, source_target_pairs={{4,0},{8,4},{12,8},{16,12},{20,16},{24,20},{28,24},{5,1},{9,5},{13... | collective-permute-start | bytes 1179656 | tf_op jit(solution)/shard_map/ppermute | solution.py:19
  1249.6 75.5 %collective-permute-start.11 = (bf16[768,256]{0,1:T(8,128)(2,1)}, bf16[768,256]{0,1:T(8,128)(2,1)}, u32[]{:S(2)}, u32[]{:S(2)}) collective-permute-start(bf16[768,256]{0,1:T(8,128)(2,1)} %get-tuple-element.47), channel_id=1, source_target_pairs={{12,0},{16,4},{20,8},{24,12},{28,16},{13,1},{17,5},{21,9},{25,13},... | collective-permute-start | bytes 1179656 | tf_op jit(solution)/shard_map/ppermute | solution.py:19
  1294.2 21.7 collective-permute-start.6
  1295.7 21.5 collective-permute-start.8
  1297.0 24.0 %collective-permute-start.7 = (bf16[768,256]{0,1:T(8,128)(2,1)S(1)}, bf16[768,256]{0,1:T(8,128)(2,1)S(1)}, u32[]{:S(2)}, u32[]{:S(2)}) collective-permute-start(bf16[768,256]{0,1:T(8,128)(2,1)S(1)} %get-tuple-element.51), channel_id=1, source_target_pairs={{8,0},{12,4},{16,8},{20,12},{24,16},{28,20},{9,1},{13,5},{17,9},{2... | collective-permute-start | bytes 1179656 | tf_op jit(solution)/shard_map/ppermute | solution.py:19
  1315.9 18.0 collective-permute-start.10
  1339.1 149.7 %reduce-scatter.12.cloned.1.call-start = ((), (), s32[]{:S(2)}) async-start(), calls=%async_computation.19 | async-start | bytes 1327104 | tf_op jit(solution)/shard_map/reduce_scatter | solution.py:314
  1342.6 213.1 %reduce-scatter.10.cloned.1.call-start = ((), (), s32[]{:S(2)}) async-start(), calls=%async_computation.18 | async-start | bytes 1327104 | tf_op jit(solution)/shard_map/reduce_scatter | solution.py:311
  1346.1 281.6 %reduce-scatter.14.cloned.1.call-start = ((), (), s32[]{:S(2)}) async-start(), calls=%async_computation.20 | async-start | bytes 2654208 | tf_op jit(solution)/shard_map/reduce_scatter | solution.py:317
  1351.9 348.1 %reduce-scatter.8.cloned.1.call-start = ((), (), s32[]{:S(2)}) async-start(), calls=%async_computation.17 | async-start | bytes 2654208 | tf_op jit(solution)/shard_map/reduce_scatter | solution.py:308
  1357.2 525.2 %reduce-scatter.18.cloned.1.call-start = ((), (), s32[]{:S(2)}) async-start(), calls=%async_computation.22 | async-start | bytes 11943936 | tf_op jit(solution)/shard_map/reduce_scatter | solution.py:235
  1371.0 694.3 %reduce-scatter.16.cloned.1.call-start = ((), (), s32[]{:S(2)}) async-start(), calls=%async_computation.21 | async-start | bytes 11943936 | tf_op jit(solution)/shard_map/reduce_scatter | solution.py:232
  1384.7 863.1 %reduce-scatter.20.cloned.1.call-start = ((), (), s32[]{:S(2)}) async-start(), calls=%async_computation.23 | async-start | bytes 11943936 | tf_op jit(solution)/shard_map/reduce_scatter | solution.py:238
  (52 other events, 678.6 us)
Sparse Core Ops, SparseCore 0:
  10.2 43.9 all-gather.9
  56.4 41.2 all-gather.11
  99.9 62.8 all-gather.13
  164.9 64.3 all-gather.15
  236.4 170.7 all-gather.23
  409.2 152.4 all-gather.17
  563.9 150.6 all-gather.19
  716.7 150.6 all-gather.21
  882.7 130.5 all-reduce.13
  1077.8 132.5 all-reduce.15
  1339.2 81.8 all-reduce.17
  1424.3 64.3 reduce-scatter.11
  1492.7 62.9 reduce-scatter.9
  1559.6 68.0 reduce-scatter.13
  1631.7 68.2 reduce-scatter.7
  1703.4 179.0 reduce-scatter.17
  1886.3 178.8 reduce-scatter.15
  2068.7 179.0 reduce-scatter.19
